TPU v7x, 512 devices: a whole 4x8x8 slice. The times are simulated.
512 devices in a mesh: bx: 32 (over z_hi, y, core), by: 16 (over x, z_lo).
Axes of the slice: x: 4, y: 8, z: 8 (z_hi: 2, z_lo: 4; z = z_hi * 4 + z_lo), core: 2. Of those that a mesh axis runs over, the one named last changes fastest.
Arguments:
- interface_velocity: float32 [3, 2048, 2048], P(None, 'bx', 'by'), may hold values from -6 to 6
- history: float32 [6, 2, 3, 64, 32, 16, 128], P(None, None, None, 'by', 'bx'), may hold values from -6 to 6
- kernel: float32 [7, 64, 32, 16, 128], P(None, 'by', 'bx'), may hold values from -6 to 6
- velocity: float32 [3, 4, 2048, 2048], P(None, None, 'bx', 'by'), may hold values from -6 to 6
- stress: float32 [6, 4, 2048, 2048], P(None, None, 'bx', 'by'), may hold values from -6 to 6
- cohesion: float32 [4, 2048, 2048], P(None, 'bx', 'by'), may hold values from 0.5 to 4
Outputs:
- velocity_new: float32 [3, 4, 2048, 2048], P(None, None, 'bx', 'by')
- stress_new: float32 [6, 4, 2048, 2048], P(None, None, 'bx', 'by')
All inputs are finite; a program needn't handle non-finite values.
Results may differ from a plain program's by a relative error of at most 0.00005.
Values sent between devices are 32-bit elements; how exact they have to be, the bound alone decides.
No kernel may reach another device: no remote copies, remote signals or barrier semaphores. Data moves between devices by JAX's collectives and lax.ppermute only.
A program may use at most 64 MiB of HBM per device.

v0:
```python
from functools import partial
import math
import jax
import jax.numpy as jnp
from jax import lax
from jax.sharding import PartitionSpec as P

COURANT = 0.3
FRICTION = 0.6
HIGHEST = lax.Precision.HIGHEST


def extended(block, sides, width):
    for axis, dim in sides:
        count = lax.axis_size(axis)
        forward = [(i, i + 1) for i in range(count - 1)]
        forward.append((count - 1, 0))
        backward = [(target, source) for source, target in forward]
        low = lax.ppermute(
            lax.slice_in_dim(block, block.shape[dim] - width, None, axis=dim), axis, forward
        )
        high = lax.ppermute(lax.slice_in_dim(block, 0, width, axis=dim), axis, backward)
        block = jnp.concatenate([low, block, high], axis=dim)
    return block


def counting(count):
    return jnp.arange(count, dtype=jnp.int32)


def phase_table(row_index, col_index, length, sign):
    product = row_index[:, None] * col_index[None, :] % length
    angle = 2.0 * math.pi / length * product.astype(jnp.float32)
    return (jnp.cos(angle), sign * jnp.sin(angle))


def conjugate(table):
    return (table[0], -table[1])


def complex_apply(pattern, real_part, imag_part, table):
    contract = partial(jnp.einsum, pattern, precision=HIGHEST)
    return (
        contract(real_part, table[0]) - contract(imag_part, table[1]),
        contract(real_part, table[1]) + contract(imag_part, table[0]),
    )


def twist(real_part, imag_part, table_real, table_imag):
    return (
        real_part * table_real - imag_part * table_imag,
        real_part * table_imag + imag_part * table_real,
    )


def dip_blocks(block):
    return lax.all_to_all(block, "by", split_axis=2, concat_axis=2, tiled=True)


def strike_modes(block):
    return lax.all_to_all(block, "bx", split_axis=4, concat_axis=4, tiled=True)


def widen(fields):
    return extended(fields, (("bx", 2), ("by", 3)), 1)


def strike_diff(padded):
    return 0.5 * (padded[..., 2:, 1:-1] - padded[..., :-2, 1:-1])


def dip_diff(padded):
    return 0.5 * (padded[..., 1:-1, 2:] - padded[..., 1:-1, :-2])


def depth_diff(layered, ghost_layer):
    above_layer = jnp.concatenate([layered[1:], jnp.zeros_like(layered[:1])], axis=0)
    below_layer = jnp.concatenate([ghost_layer[None], layered[:-1]], axis=0)
    return 0.5 * (above_layer - below_layer)


def yield_limit(trial_stress, cohesion):
    pressure = (trial_stress[0] + trial_stress[1] + trial_stress[2]) / 3.0
    normal_dev = trial_stress[:3] - pressure[None]
    second = 0.5 * jnp.sum(normal_dev * normal_dev, axis=0) + jnp.sum(
        trial_stress[3:] * trial_stress[3:], axis=0
    )
    shear_stress = jnp.sqrt(second)
    yield_stress = cohesion + FRICTION * jnp.maximum(-pressure, 0.0)
    factor = yield_stress / jnp.maximum(shear_stress, yield_stress)
    return jnp.concatenate(
        [pressure[None] + factor[None] * normal_dev, factor[None] * trial_stress[3:]], axis=0
    )


def advance_bulk(velocity, stress, traction, interface_velocity, cohesion):
    padded_stress = widen(stress)
    forcing = jnp.stack(
        [
            strike_diff(padded_stress[0])
            + dip_diff(padded_stress[3])
            + depth_diff(stress[4], traction[0]),
            strike_diff(padded_stress[3])
            + dip_diff(padded_stress[1])
            + depth_diff(stress[5], traction[1]),
            strike_diff(padded_stress[4])
            + dip_diff(padded_stress[5])
            + depth_diff(stress[2], traction[2]),
        ]
    )
    velocity_new = velocity + COURANT * forcing
    padded_velocity = widen(velocity_new)
    strike_grad = strike_diff(padded_velocity)
    dip_grad = dip_diff(padded_velocity)
    depth_grad = jnp.stack(
        [
            depth_diff(velocity_new[component], interface_velocity[component])
            for component in range(3)
        ]
    )
    dilation = strike_grad[0] + dip_grad[1] + depth_grad[2]
    rates = jnp.stack(
        [
            dilation + 2.0 * strike_grad[0],
            dilation + 2.0 * dip_grad[1],
            dilation + 2.0 * depth_grad[2],
            dip_grad[0] + strike_grad[1],
            depth_grad[0] + strike_grad[2],
            depth_grad[1] + dip_grad[2],
        ]
    )
    trial_stress = stress + COURANT * rates
    return (velocity_new, yield_limit(trial_stress, cohesion))


def local(interface_velocity, history, kernel, velocity, stress, cohesion):
    strike_count = lax.axis_size("bx")
    dip_count = lax.axis_size("by")
    strike_index = lax.axis_index("bx")
    strike_cells = interface_velocity.shape[1]
    dip_cells = interface_velocity.shape[2]
    row_block = dip_cells // strike_count
    mode_block = strike_cells // dip_count
    strike_length = strike_cells * strike_count
    dip_length = dip_cells * dip_count
    scale = 1.0 / math.sqrt(strike_length * dip_length)
    strike_table = phase_table(counting(strike_count), counting(strike_count), strike_count, -1.0)
    strike_twist = phase_table(counting(strike_cells), counting(strike_count), strike_length, -1.0)
    cell_table = phase_table(counting(strike_cells), counting(strike_cells), strike_cells, -1.0)
    dip_table = phase_table(counting(dip_count), counting(dip_count), dip_count, -1.0)
    column_table = phase_table(counting(dip_cells), counting(dip_cells), dip_cells, -1.0)
    gathered = lax.all_gather(interface_velocity, "bx", axis=1, tiled=True)
    own_columns = lax.dynamic_slice_in_dim(gathered, strike_index * row_block, row_block, 2)
    grouped = own_columns.reshape(3, strike_count, strike_cells, row_block)
    first_pattern = "cpqr,pk->cqkr"
    real_part = jnp.einsum(first_pattern, grouped, strike_table[0], precision=HIGHEST)
    imag_part = jnp.einsum(first_pattern, grouped, strike_table[1], precision=HIGHEST)
    real_part, imag_part = twist(
        real_part, imag_part, strike_twist[0][None, :, :, None], strike_twist[1][None, :, :, None]
    )
    real_part, imag_part = complex_apply("cqkr,qm->cmkr", real_part, imag_part, cell_table)
    stacked = jnp.stack([real_part, imag_part])
    dip_offsets = row_block * strike_index + counting(row_block)
    dip_twist = phase_table(counting(dip_count), dip_offsets, dip_length, -1.0)
    arrived = dip_blocks(stacked.reshape(2, 3, strike_cells, dip_cells))
    arrived = arrived.reshape(2, 3, dip_count, mode_block, strike_count, row_block)
    real_part, imag_part = complex_apply("cjukr,jl->clukr", arrived[0], arrived[1], dip_table)
    real_part, imag_part = twist(
        real_part,
        imag_part,
        dip_twist[0][None, :, None, None, :],
        dip_twist[1][None, :, None, None, :],
    )
    arrived = strike_modes(
        jnp.stack([real_part, imag_part]).reshape(2, 3, dip_count, mode_block, dip_cells)
    )
    real_part, imag_part = (arrived[0], arrived[1])
    real_part, imag_part = complex_apply("clus,sm->culm", real_part, imag_part, column_table)
    spectrum = scale * jnp.stack([real_part, imag_part])[:, :, :, None]
    past_terms = jnp.einsum("hupks,hzcupks->zcupks", kernel[1:], history, precision=HIGHEST)
    response = kernel[0][None, None] * spectrum + past_terms
    real_part, imag_part = complex_apply(
        "cuks,sm->ckum", response[0, :, :, 0], response[1, :, :, 0], conjugate(column_table)
    )
    dip_offsets = row_block * strike_index + counting(row_block)
    back_twist = conjugate(phase_table(counting(dip_count), dip_offsets, dip_length, -1.0))
    arrived = strike_modes(jnp.stack([real_part, imag_part]))
    arrived = arrived.reshape(2, 3, dip_count, mode_block, strike_count, row_block)
    real_part, imag_part = twist(
        arrived[0],
        arrived[1],
        back_twist[0][None, :, None, None, :],
        back_twist[1][None, :, None, None, :],
    )
    real_part, imag_part = complex_apply(
        "clukr,lj->cjukr", real_part, imag_part, conjugate(dip_table)
    )
    arrived = dip_blocks(jnp.stack([real_part, imag_part]).reshape(2, 3, strike_cells, dip_cells))
    arrived = arrived.reshape(2, 3, strike_cells, strike_count, row_block)
    real_part, imag_part = complex_apply(
        "cmkr,mq->cqkr", arrived[0], arrived[1], conjugate(cell_table)
    )
    back_strike = conjugate(strike_twist)
    real_part, imag_part = twist(
        real_part, imag_part, back_strike[0][None, :, :, None], back_strike[1][None, :, :, None]
    )
    inverse_table = conjugate(strike_table)
    spatial = jnp.einsum(
        "cqkr,kp->cpqr", real_part, inverse_table[0], precision=HIGHEST
    ) - jnp.einsum("cqkr,kp->cpqr", imag_part, inverse_table[1], precision=HIGHEST)
    gathered = lax.all_gather(
        spatial.reshape(3, strike_length, row_block), "bx", axis=2, tiled=True
    )
    traction = scale * lax.dynamic_slice_in_dim(
        gathered, strike_index * strike_cells, strike_cells, 1
    )
    velocity_new, stress_new = advance_bulk(
        velocity, stress, traction, interface_velocity, cohesion
    )
    return (velocity_new, stress_new)


def solution(mesh):
    return jax.shard_map(
        local,
        mesh=mesh,
        in_specs=(
            P(None, "bx", "by"),
            P(None, None, None, "by", "bx", None, None),
            P(None, "by", "bx", None, None),
            P(None, None, "bx", "by"),
            P(None, None, "bx", "by"),
            P(None, "bx", "by"),
        ),
        out_specs=(P(None, None, "bx", "by"), P(None, None, "bx", "by")),
        check_vma=False,
    )
```

profile of v0, /device:TPU:6, one launch (start us, length us, event | category | flops | bytes accessed | tf_op | source)
XLA Modules:
  0.0 402.0 jit_solution(16210227547957793094)
XLA Ops:
  8.0 108.7 %all-gather.3.cloned.1.call-done = f32[3,2048,128]{2,1,0:T(8,128)} async-done(((f32[3,64,128]{2,1,0:T(8,128)}), f32[3,2048,128]{2,1,0:T(8,128)}) %all-gather.3.cloned.1.call-update) | async-done | bytes 3145744 | tf_op jit(solution)/shard_map/all_gather | solution.py:152
  116.7 2.8 constant_dynamic-slice_fusion
  119.5 1.3 copy.226
  124.5 5.9 %all-to-all-start = ((f32[2,3,64,128]{3,0,1,2:T(2,128)}), f32[2,3,64,128]{3,0,1,2:T(2,128)S(1)}, u32[]{:S(2)}, u32[]{:S(2)}) async-start(f32[2,3,64,128]{3,0,1,2:T(2,128)} %copy.159), calls=%async_computation | async-start | bytes 393216 | tf_op jit(solution)/shard_map/all_to_all | solution.py:57
  131.8 6.1 %all-to-all-done = f32[2,3,64,128]{3,0,1,2:T(2,128)S(1)} async-done(((f32[2,3,64,128]{3,0,1,2:T(2,128)}), f32[2,3,64,128]{3,0,1,2:T(2,128)S(1)}, u32[]{:S(2)}, u32[]{:S(2)}) %all-to-all-start) | async-done | bytes 196640 | tf_op jit(solution)/shard_map/all_to_all | solution.py:57
  139.0 3.4 reshape.256
  142.4 1.6 copy.161
  144.0 1.3 fusion.149
  146.6 4.2 %reshape.257 = f32[3,16,4,32,4]{4,3,0,2,1:T(8,128)S(1)} reshape(f32[3,64,128]{2,0,1:T(4,128)} %get-tuple-element.10) | data formatting | bytes 196608 | tf_op jit(solution)/shard_map/squeeze | solution.py:167
  150.8 1.6 copy.163
  152.4 1.5 convolution_add_fusion.1
  153.9 1.6 subtract_bitcast_fusion
  157.4 1.9 reshape.260
  159.3 6.0 %all-to-all-start.1 = ((f32[32,1,1536]{2,1,0:T(1,128)}), f32[32,1,1536]{2,1,0:T(1,128)S(1)}, u32[]{:S(2)}, u32[]{:S(2)}) async-start(f32[32,1,1536]{2,1,0:T(1,128)} %reshape.260), calls=%async_computation.1 | async-start | bytes 393216 | tf_op jit(solution)/shard_map/all_to_all | solution.py:61
  165.4 1.4 multiply_bitcast_fusion
  166.8 14.2 %all-to-all-done.1 = f32[32,1,1536]{2,1,0:T(1,128)S(1)} async-done(((f32[32,1,1536]{2,1,0:T(1,128)}), f32[32,1,1536]{2,1,0:T(1,128)S(1)}, u32[]{:S(2)}, u32[]{:S(2)}) %all-to-all-start.1) | async-done | bytes 196640 | tf_op jit(solution)/shard_map/all_to_all | solution.py:61
  190.7 18.9 %all_to_all.20 = f32[32,1,1536]{2,1,0:T(1,128)S(1)} all-to-all(f32[32,1,1536]{2,1,0:T(1,128)S(1)} %reshape.262), channel_id=1, replica_groups=mesh['bx'=32,'by'=16] {'bx'}, dimensions={0} | all-to-all | bytes 393216 | tf_op jit(solution)/shard_map/all_to_all | solution.py:61
  213.8 1.3 fusion.146
  215.3 1.3 fusion.1
  216.6 2.2 copy.176
  218.8 3.2 stack.88
  222.1 1.5 fusion
  223.6 1.3 copy.179
  224.9 2.6 stack.89
  228.4 5.8 %all-to-all-start.3 = ((f32[2,3,64,128]{3,0,1,2:T(2,128)}), f32[2,3,64,128]{3,0,1,2:T(2,128)S(1)}, u32[]{:S(2)}, u32[]{:S(2)}) async-start(f32[2,3,64,128]{3,0,1,2:T(2,128)} %copy.180), calls=%async_computation.3 | async-start | bytes 393216 | tf_op jit(solution)/shard_map/all_to_all | solution.py:57
  234.5 6.3 %all-to-all-done.3 = f32[2,3,64,128]{3,0,1,2:T(2,128)S(1)} async-done(((f32[2,3,64,128]{3,0,1,2:T(2,128)}), f32[2,3,64,128]{3,0,1,2:T(2,128)S(1)}, u32[]{:S(2)}, u32[]{:S(2)}) %all-to-all-start.3) | async-done | bytes 196640 | tf_op jit(solution)/shard_map/all_to_all | solution.py:57
  244.8 1.9 collective-permute-start
  246.8 9.7 %collective-permute-start.1 = (f32[6,4,1,128]{3,1,2,0:T(4,128)S(1)}, f32[6,4,1,128]{3,1,2,0:T(4,128)S(1)}, u32[]{:S(2)}, u32[]{:S(2)}) collective-permute-start(f32[6,4,1,128]{3,1,2,0:T(4,128)S(1)} %bitcast.319), channel_id=1, source_target_pairs={{16,0},{32,16},{48,32},{64,48},{80,64},{96,80},{112,96},{128,112},... | collective-permute-start | bytes 36872 | tf_op jit(solution)/shard_map/ppermute | solution.py:22
  257.9 1.5 copy.154
  260.3 2.7 collective-permute-start.2
  263.0 5.9 %collective-permute-start.3 = (f32[6,4,66,1]{2,1,3,0:T(4,128)S(1)}, f32[6,4,66,1]{2,1,3,0:T(4,128)S(1)}, u32[]{:S(2)}, u32[]{:S(2)}) collective-permute-start(f32[6,4,66,1]{2,1,3,0:T(4,128)S(1)} %get-tuple-element.20), channel_id=1, source_target_pairs={{1,0},{2,1},{3,2},{4,3},{5,4},{6,5},{7,6},{8,7},{9,8},{10,9},{11,1... | collective-permute-start | bytes 19016 | tf_op jit(solution)/shard_map/ppermute | solution.py:22
  270.1 2.1 copy.193
  272.3 2.5 maximum_bitcast_fusion.2
  274.7 1.8 maximum_bitcast_fusion.3
  276.6 68.3 %all-gather.5.cloned.1.call-done = f32[3,2048,128]{1,0,2:T(4,128)} async-done(((f32[3,2048,4]{1,0,2:T(4,128)}), f32[3,2048,128]{1,0,2:T(4,128)}) %all-gather.5.cloned.1.call-update) | async-done | bytes 3145744 | tf_op jit(solution)/shard_map/all_gather | solution.py:211
  346.1 1.9 fusion.27
  349.6 1.3 fusion.319
  350.9 1.4 copy.194
  352.4 1.9 collective-permute-start.4
  355.2 2.4 collective-permute-start.5
  359.7 6.7 %collective-permute-done.5 = f32[3,4,1,128]{3,1,2,0:T(4,128)} collective-permute-done((f32[3,4,1,128]{3,1,2,0:T(4,128)}, f32[3,4,1,128]{3,1,2,0:T(4,128)}, u32[]{:S(2)}, u32[]{:S(2)}) %collective-permute-start.5) | collective-permute-done | bytes 6176 | tf_op jit(solution)/shard_map/ppermute | solution.py:19
  366.4 1.9 copy.197
  368.3 1.4 pad_maximum_fusion.22
  369.7 5.9 %collective-permute-start.6 = (f32[3,4,66,1]{2,1,3,0:T(4,128)}, f32[3,4,66,1]{2,1,3,0:T(4,128)S(1)}, u32[]{:S(2)}, u32[]{:S(2)}) collective-permute-start(f32[3,4,66,1]{2,1,3,0:T(4,128)} %get-tuple-element.23), channel_id=1, source_target_pairs={{1,0},{2,1},{3,2},{4,3},{5,4},{6,5},{7,6},{8,7},{9,8},{10,9},{11,1... | collective-permute-start | bytes 9512 | tf_op jit(solution)/shard_map/ppermute | solution.py:22
  375.6 2.2 collective-permute-start.7
  380.0 4.0 %collective-permute-done.7 = f32[3,4,66,1]{2,1,3,0:T(4,128)S(1)} collective-permute-done((f32[3,4,66,1]{2,1,3,0:T(4,128)}, f32[3,4,66,1]{2,1,3,0:T(4,128)S(1)}, u32[]{:S(2)}, u32[]{:S(2)}) %collective-permute-start.7) | collective-permute-done | bytes 3200 | tf_op jit(solution)/shard_map/ppermute | solution.py:19
  384.1 4.8 %fusion.11 = (f32[3,4,64,128]{2,1,3,0:T(4,128)S(1)}, f32[3,4,64,128]{2,1,3,0:T(4,128)S(1)}) fusion(f32[3,4,66,1]{2,1,3,0:T(4,128)S(1)} %collective-permute-done.7, f32[3,4,1,128]{2,1,3,0:T(4,128)S(1)} %copy.195, f32[3,4,64,128]{2,1,3,0:T(4,128)S(1)} %fusion.14, f32[3,4,1,128]{2,1,3,0:T(4,128)} %copy.197, f32[3,4,66,1]{2,1,3,0:T(4,128)S(1)} %collective-permute-done.6), kind=kLoop, calls=%fused_computation.32 | loop fusion | flops 1179648 | bytes 1198272 | tf_op jit(solution)/shard_map/mul | solution.py:73
  393.2 1.4 copy.206
  (154 shorter events, 45.1 us)
Async XLA Ops:
  7.2 109.5 %all-gather.3.cloned.1.call-start = ((), (), s32[]{:S(2)}) async-start(), calls=%async_computation.4 | async-start | bytes 3244032 | tf_op jit(solution)/shard_map/all_gather | solution.py:152
  123.1 8.1 %copy-start.20 = (f32[7,4,1,16,128]{4,3,2,1,0:T(8,128)S(1)}, f32[7,4,1,16,128]{4,3,2,1,0:T(8,128)}, u32[]{:S(2)}) copy-start(f32[7,4,1,16,128]{4,3,2,1,0:T(8,128)} %param.8) | copy-start | bytes 688132
  124.5 13.4 %all-to-all-start = ((f32[2,3,64,128]{3,0,1,2:T(2,128)}), f32[2,3,64,128]{3,0,1,2:T(2,128)S(1)}, u32[]{:S(2)}, u32[]{:S(2)}) async-start(f32[2,3,64,128]{3,0,1,2:T(2,128)} %copy.159), calls=%async_computation | async-start | bytes 393216 | tf_op jit(solution)/shard_map/all_to_all | solution.py:57
  157.4 7.9 %copy-start.5 = (f32[6,2,3,4,1,16,128]{6,5,4,3,2,1,0:T(8,128)S(1)}, f32[6,2,3,4,1,16,128]{6,5,4,3,2,1,0:T(8,128)}, u32[]{:S(2)}) copy-start(f32[6,2,3,4,1,16,128]{6,5,4,3,2,1,0:T(8,128)} %param.7) | copy-start | bytes 3538948
  157.4 7.9 %copy-start.16 = (f32[4,16,128,6]{2,1,0,3:T(8,128)S(1)}, f32[4,16,128,6]{2,1,0,3:T(8,128)}, u32[]{:S(2)}) copy-start(f32[4,16,128,6]{2,1,0,3:T(8,128)} %slice_bitcast_fusion.14) | copy-start | bytes 589828
  159.3 21.7 %all-to-all-start.1 = ((f32[32,1,1536]{2,1,0:T(1,128)}), f32[32,1,1536]{2,1,0:T(1,128)S(1)}, u32[]{:S(2)}, u32[]{:S(2)}) async-start(f32[32,1,1536]{2,1,0:T(1,128)} %reshape.260), calls=%async_computation.1 | async-start | bytes 393216 | tf_op jit(solution)/shard_map/all_to_all | solution.py:61
  184.0 2.6 copy-start.22
  212.1 0.7 copy-start.23
  212.1 0.7 copy-start.24
  224.9 2.6 copy-start.17
  228.4 12.4 %all-to-all-start.3 = ((f32[2,3,64,128]{3,0,1,2:T(2,128)}), f32[2,3,64,128]{3,0,1,2:T(2,128)S(1)}, u32[]{:S(2)}, u32[]{:S(2)}) async-start(f32[2,3,64,128]{3,0,1,2:T(2,128)} %copy.180), calls=%async_computation.3 | async-start | bytes 393216 | tf_op jit(solution)/shard_map/all_to_all | solution.py:57
  234.2 110.7 %all-gather.5.cloned.1.call-start = ((), (), s32[]{:S(2)}) async-start(), calls=%async_computation.5 | async-start | bytes 4325376 | tf_op jit(solution)/shard_map/all_gather | solution.py:211
  242.2 2.6 copy-start.15
  244.8 12.3 %collective-permute-start = (f32[6,4,1,128]{3,1,2,0:T(4,128)S(1)}, f32[6,4,1,128]{3,1,2,0:T(4,128)S(1)}, u32[]{:S(2)}, u32[]{:S(2)}) collective-permute-start(f32[6,4,1,128]{3,1,2,0:T(4,128)S(1)} %bitcast.320), channel_id=1, source_target_pairs={{0,16},{16,32},{32,48},{48,64},{64,80},{80,96},{96,112},{112,128},... | collective-permute-start | bytes 36872 | tf_op jit(solution)/shard_map/ppermute | solution.py:19
  246.8 11.2 %collective-permute-start.1 = (f32[6,4,1,128]{3,1,2,0:T(4,128)S(1)}, f32[6,4,1,128]{3,1,2,0:T(4,128)S(1)}, u32[]{:S(2)}, u32[]{:S(2)}) collective-permute-start(f32[6,4,1,128]{3,1,2,0:T(4,128)S(1)} %bitcast.319), channel_id=1, source_target_pairs={{16,0},{32,16},{48,32},{64,48},{80,64},{96,80},{112,96},{128,112},... | collective-permute-start | bytes 36872 | tf_op jit(solution)/shard_map/ppermute | solution.py:22
  260.3 12.0 %collective-permute-start.2 = (f32[6,4,66,1]{2,1,3,0:T(4,128)S(1)}, f32[6,4,66,1]{2,1,3,0:T(4,128)S(1)}, u32[]{:S(2)}, u32[]{:S(2)}) collective-permute-start(f32[6,4,66,1]{2,1,3,0:T(4,128)S(1)} %get-tuple-element.19), channel_id=1, source_target_pairs={{0,1},{1,2},{2,3},{3,4},{4,5},{5,6},{6,7},{7,8},{8,9},{9,10},{10,1... | collective-permute-start | bytes 19016 | tf_op jit(solution)/shard_map/ppermute | solution.py:19
  263.0 9.3 %collective-permute-start.3 = (f32[6,4,66,1]{2,1,3,0:T(4,128)S(1)}, f32[6,4,66,1]{2,1,3,0:T(4,128)S(1)}, u32[]{:S(2)}, u32[]{:S(2)}) collective-permute-start(f32[6,4,66,1]{2,1,3,0:T(4,128)S(1)} %get-tuple-element.20), channel_id=1, source_target_pairs={{1,0},{2,1},{3,2},{4,3},{5,4},{6,5},{7,6},{8,7},{9,8},{10,9},{11,1... | collective-permute-start | bytes 19016 | tf_op jit(solution)/shard_map/ppermute | solution.py:22
  272.2 2.5 copy-start
  276.5 71.5 %copy-start.3 = (f32[4,66,130]{1,0,2:T(4,128)S(1)}, f32[4,66,130]{1,0,2:T(4,128)}, u32[]{:S(2)}) copy-start(f32[4,66,130]{1,0,2:T(4,128)} %get-tuple-element.14) | copy-start | bytes 411844
  276.5 71.6 %copy-start.4 = (f32[4,66,130]{1,0,2:T(4,128)S(1)}, f32[4,66,130]{1,0,2:T(4,128)}, u32[]{:S(2)}) copy-start(f32[4,66,130]{1,0,2:T(4,128)} %get-tuple-element.16) | copy-start | bytes 411844
  276.5 71.6 %copy-start.11 = (f32[3,64,128]{1,0,2:T(4,128)S(1)}, f32[3,64,128]{1,0,2:T(4,128)}, u32[]{:S(2)}) copy-start(f32[3,64,128]{1,0,2:T(4,128)} %get-tuple-element.29) | copy-start | bytes 294916
  276.5 71.6 %copy-start.12 = (f32[3,64,128]{1,0,2:T(4,128)S(1)}, f32[3,64,128]{1,0,2:T(4,128)}, u32[]{:S(2)}) copy-start(f32[3,64,128]{1,0,2:T(4,128)} %get-tuple-element.32) | copy-start | bytes 294916
  276.5 71.6 %copy-start.13 = (f32[3,64,128]{1,0,2:T(4,128)S(1)}, f32[3,64,128]{1,0,2:T(4,128)}, u32[]{:S(2)}) copy-start(f32[3,64,128]{1,0,2:T(4,128)} %get-tuple-element.33) | copy-start | bytes 294916
  276.6 71.6 %copy-start.14 = (f32[3,64,128]{1,0,2:T(4,128)S(1)}, f32[3,64,128]{1,0,2:T(4,128)}, u32[]{:S(2)}) copy-start(f32[3,64,128]{1,0,2:T(4,128)} %get-tuple-element.34) | copy-start | bytes 294916
  348.1 1.1 copy-start.1
  350.9 6.6 %copy-start.18 = (f32[3,64,128]{2,1,0:T(8,128)S(1)}, f32[3,64,128]{2,1,0:T(8,128)}, u32[]{:S(2)}) copy-start(f32[3,64,128]{2,1,0:T(8,128)} %param.6) | copy-start | bytes 294916
  350.9 7.6 %copy-start.21 = (f32[4,64,128]{2,1,0:T(8,128)S(1)}, f32[4,64,128]{2,1,0:T(8,128)}, u32[]{:S(2)}) copy-start(f32[4,64,128]{2,1,0:T(8,128)} %param.11) | copy-start | bytes 393220
  352.4 7.0 %collective-permute-start.4 = (f32[3,4,1,128]{3,1,2,0:T(4,128)S(1)}, f32[3,4,1,128]{3,1,2,0:T(4,128)S(1)}, u32[]{:S(2)}, u32[]{:S(2)}) collective-permute-start(f32[3,4,1,128]{3,1,2,0:T(4,128)S(1)} %copy.194), channel_id=1, source_target_pairs={{16,0},{32,16},{48,32},{64,48},{80,64},{96,80},{112,96},{128,112},... | collective-permute-start | bytes 18440 | tf_op jit(solution)/shard_map/ppermute | solution.py:22
  355.2 11.3 %collective-permute-start.5 = (f32[3,4,1,128]{3,1,2,0:T(4,128)}, f32[3,4,1,128]{3,1,2,0:T(4,128)}, u32[]{:S(2)}, u32[]{:S(2)}) collective-permute-start(f32[3,4,1,128]{3,1,2,0:T(4,128)} %copy.196), channel_id=1, source_target_pairs={{0,16},{16,32},{32,48},{48,64},{64,80},{80,96},{96,112},{112,128},... | collective-permute-start | bytes 18440 | tf_op jit(solution)/shard_map/ppermute | solution.py:19
  369.7 10.3 %collective-permute-start.6 = (f32[3,4,66,1]{2,1,3,0:T(4,128)}, f32[3,4,66,1]{2,1,3,0:T(4,128)S(1)}, u32[]{:S(2)}, u32[]{:S(2)}) collective-permute-start(f32[3,4,66,1]{2,1,3,0:T(4,128)} %get-tuple-element.23), channel_id=1, source_target_pairs={{1,0},{2,1},{3,2},{4,3},{5,4},{6,5},{7,6},{8,7},{9,8},{10,9},{11,1... | collective-permute-start | bytes 9512 | tf_op jit(solution)/shard_map/ppermute | solution.py:22
  375.6 8.4 %collective-permute-start.7 = (f32[3,4,66,1]{2,1,3,0:T(4,128)}, f32[3,4,66,1]{2,1,3,0:T(4,128)S(1)}, u32[]{:S(2)}, u32[]{:S(2)}) collective-permute-start(f32[3,4,66,1]{2,1,3,0:T(4,128)} %get-tuple-element.24), channel_id=1, source_target_pairs={{0,1},{1,2},{2,3},{3,4},{4,5},{5,6},{6,7},{7,8},{8,9},{9,10},{10,1... | collective-permute-start | bytes 9512 | tf_op jit(solution)/shard_map/ppermute | solution.py:19
  380.0 8.8 %copy-start.2 = (f32[3,64,128]{1,0,2:T(4,128)S(1)}, f32[3,64,128]{1,0,2:T(4,128)}, u32[]{:S(2)}) copy-start(f32[3,64,128]{1,0,2:T(4,128)} %get-tuple-element.46) | copy-start | bytes 294916
  389.1 1.0 copy-start.8
  389.1 1.0 copy-start.9
  389.1 1.0 copy-start.19
  389.3 1.1 copy-start.6
  389.3 1.1 copy-start.7
  391.2 1.0 copy-start.10
Sparse Core Ops, SparseCore 0:
  11.4 105.2 all-gather.2
  244.9 99.8 all-gather.4
where the time goes:
time: 407 us; the launch traced here: 402 us
  waiting for transfers between devices  215 us (53%)
  local copies, waits for them, and re-layouts  58.5 us (14%)
  starting transfers between devices  50.5 us (12%)
  other arithmetic  24.1 us (6%)
  matrix products  19.5 us (5%)
  blocking collectives  18.9 us (5%)
  between operations  15.5 us (4%)
    all_gather x1, waiting for transfers between devices, local(): gathered = lax.all_gather(interface_velocity, 'bx', axis=1, tiled=True)  109 us
    all_gather x1, waiting for transfers between devices, local(): lax.all_gather(spatial.reshape(3, strike_length, row_block), 'bx', axis=2...  68.3 us
    ppermute x4, starting transfers between devices, extended(): lax.ppermute(lax.slice_in_dim(block, 0, width, axis=dim), axis, backward)  23.4 us
    all_to_all x1, blocking collectives, strike_modes(): return lax.all_to_all(block, 'bx', split_axis=4, concat_axis=4, tiled=True)  18.9 us
    unnamed x66, local copies, waits for them, and re-layouts  14.5 us
    all_to_all x1, waiting for transfers between devices, strike_modes(): return lax.all_to_all(block, 'bx', split_axis=4, concat_axis=4, tiled=True)  14.2 us
    all_to_all x2, waiting for transfers between devices, dip_blocks(): return lax.all_to_all(block, 'by', split_axis=2, concat_axis=2, tiled=True)  12.4 us
    all_to_all x2, starting transfers between devices, dip_blocks(): return lax.all_to_all(block, 'by', split_axis=2, concat_axis=2, tiled=True)  11.6 us
  transfers between devices with their start and end apart: 13, of which 7 were waited for; matrix products, arithmetic and copies ran while one was open for 5% of the time, Pallas kernels for 0%

commit v1 on v0

--- a/solution.py
+++ b/solution.py
@@ -58,7 +58,9 @@
 
 
 def strike_modes(block):
-    return lax.all_to_all(block, "bx", split_axis=4, concat_axis=4, tiled=True)
+    return jnp.concatenate(
+        lax.all_to_all(jnp.stack(jnp.split(block, lax.axis_size("bx"), axis=4)), "bx", 0, 0), axis=4
+    )
 
 
 def widen(fields):

time: 407 us -> 441 us (1.084)
  other arithmetic: 24.1 us -> 49.6 us
  local copies, waits for them, and re-layouts: 58.5 us -> 63.2 us
    unnamed x5 -> x67, other arithmetic: 0.93 us -> 26.3 us
    another operation x2 -> x1, local copies, waits for them, and re-layouts: 1.75 us -> 6.47 us  [strike_modes(): jnp.stack(jnp.split(block, lax.axis_size('bx'), axis=4))]
    unnamed x66 -> x60, local copies, waits for them, and re-layouts: 14.5 us -> 13.8 us
  transfers between devices with their start and end apart: 13 -> 13, of which waited for: 7 -> 7; matrix products, arithmetic and copies ran while one was open for 5% -> 4% of each run, Pallas kernels for 0% -> 0%
where the time goes in v1:
time: 441 us; the launch traced here: 436 us
  waiting for transfers between devices  216 us (49%)
  local copies, waits for them, and re-layouts  63.2 us (14%)
  starting transfers between devices  50.1 us (11%)
  other arithmetic  49.6 us (11%)
  matrix products  23 us (5%)
  blocking collectives  19.1 us (4%)
  between operations  15.3 us (3%)
    all_gather x1, waiting for transfers between devices, local(): gathered = lax.all_gather(interface_velocity, 'bx', axis=1, tiled=True)  109 us
    all_gather x1, waiting for transfers between devices, local(): lax.all_gather(spatial.reshape(3, strike_length, row_block), 'bx', axis=2...  68.3 us
    unnamed x67, other arithmetic  26.3 us
    ppermute x4, starting transfers between devices, extended(): lax.ppermute(lax.slice_in_dim(block, 0, width, axis=dim), axis, backward)  23.4 us
    all_to_all x1, blocking collectives, strike_modes(): lax.all_to_all(jnp.stack(jnp.split(block, lax.axis_size('bx'), axis=4)),...  19.1 us
    all_to_all x1, waiting for transfers between devices, strike_modes(): lax.all_to_all(jnp.stack(jnp.split(block, lax.axis_size('bx'), axis=4)),...  14.8 us
    unnamed x60, local copies, waits for them, and re-layouts  13.8 us
    all_to_all x2, waiting for transfers between devices, dip_blocks(): return lax.all_to_all(block, 'by', split_axis=2, concat_axis=2, tiled=True)  12.4 us
  transfers between devices with their start and end apart: 13, of which 7 were waited for; matrix products, arithmetic and copies ran while one was open for 4% of the time, Pallas kernels for 0%

profile of v1, /device:TPU:6, one launch (start us, length us, event | category | flops | bytes accessed | tf_op | source)
XLA Modules:
  0.0 436.0 jit_solution(15239852054889276096)
XLA Ops:
  8.0 108.7 %all-gather.3.cloned.1.call-done = f32[3,2048,128]{2,1,0:T(8,128)} async-done(((f32[3,64,128]{2,1,0:T(8,128)}), f32[3,2048,128]{2,1,0:T(8,128)}) %all-gather.3.cloned.1.call-update) | async-done | bytes 3145744 | tf_op jit(solution)/shard_map/all_gather | solution.py:154
  116.7 2.8 constant_dynamic-slice_fusion
  124.5 5.5 %all-to-all-start = ((f32[2,3,64,128]{3,0,1,2:T(2,128)}), f32[2,3,64,128]{3,0,1,2:T(2,128)S(1)}, u32[]{:S(2)}, u32[]{:S(2)}) async-start(f32[2,3,64,128]{3,0,1,2:T(2,128)} %copy.394), calls=%async_computation | async-start | bytes 393216 | tf_op jit(solution)/shard_map/all_to_all | solution.py:57
  131.5 6.1 %all-to-all-done = f32[2,3,64,128]{3,0,1,2:T(2,128)S(1)} async-done(((f32[2,3,64,128]{3,0,1,2:T(2,128)}), f32[2,3,64,128]{3,0,1,2:T(2,128)S(1)}, u32[]{:S(2)}, u32[]{:S(2)}) %all-to-all-start) | async-done | bytes 196640 | tf_op jit(solution)/shard_map/all_to_all | solution.py:57
  138.7 3.4 reshape.264
  142.1 1.6 copy.396
  146.2 4.2 reshape.265
  150.4 1.6 copy.398
  152.0 1.5 convolution_add_fusion.1
  153.6 1.6 subtract_bitcast_fusion
  156.8 1.9 reshape.268
  158.7 6.0 %all-to-all-start.1 = ((f32[32,1,1536]{2,1,0:T(1,128)}), f32[32,1,1536]{2,1,0:T(1,128)S(1)}, u32[]{:S(2)}, u32[]{:S(2)}) async-start(f32[32,1,1536]{2,1,0:T(1,128)} %reshape.268), calls=%async_computation.1 | async-start | bytes 393216 | tf_op jit(solution)/shard_map/all_to_all | solution.py:62
  165.6 14.8 %all-to-all-done.1 = f32[32,1,1536]{2,1,0:T(1,128)S(1)} async-done(((f32[32,1,1536]{2,1,0:T(1,128)}), f32[32,1,1536]{2,1,0:T(1,128)S(1)}, u32[]{:S(2)}, u32[]{:S(2)}) %all-to-all-start.1) | async-done | bytes 196640 | tf_op jit(solution)/shard_map/all_to_all | solution.py:62
  183.9 1.4 fusion.166
  185.3 1.4 fusion.160
  186.9 1.4 fusion.9
  188.3 1.4 fusion.8
  217.2 6.5 %copy.409 = f32[32,2,3,16,4,4]{3,5,4,2,1,0:T(4,128)S(1)} copy(f32[32,2,3,16,4,4]{5,3,4,2,1,0:T(8,128)} %fusion.132) | data formatting | bytes 393216 | tf_op jit(solution)/shard_map/stack | solution.py:62
  224.9 19.1 %all_to_all.20 = f32[32,1,1536]{2,1,0:T(1,128)S(1)} all-to-all(f32[32,1,1536]{2,1,0:T(1,128)S(1)} %reshape.270), channel_id=1, replica_groups=mesh['bx'=32,'by'=16] {'bx'}, dimensions={0} | all-to-all | bytes 393216 | tf_op jit(solution)/shard_map/all_to_all | solution.py:62
  251.0 2.2 copy.413
  253.2 3.2 stack.352
  256.4 1.5 fusion
  258.0 1.3 copy.416
  259.3 2.6 stack.353
  262.8 5.8 %all-to-all-start.3 = ((f32[2,3,64,128]{3,0,1,2:T(2,128)}), f32[2,3,64,128]{3,0,1,2:T(2,128)S(1)}, u32[]{:S(2)}, u32[]{:S(2)}) async-start(f32[2,3,64,128]{3,0,1,2:T(2,128)} %copy.417), calls=%async_computation.3 | async-start | bytes 393216 | tf_op jit(solution)/shard_map/all_to_all | solution.py:57
  268.8 6.4 %all-to-all-done.3 = f32[2,3,64,128]{3,0,1,2:T(2,128)S(1)} async-done(((f32[2,3,64,128]{3,0,1,2:T(2,128)}), f32[2,3,64,128]{3,0,1,2:T(2,128)S(1)}, u32[]{:S(2)}, u32[]{:S(2)}) %all-to-all-start.3) | async-done | bytes 196640 | tf_op jit(solution)/shard_map/all_to_all | solution.py:57
  279.2 1.9 collective-permute-start
  281.1 9.7 %collective-permute-start.1 = (f32[6,4,1,128]{3,1,2,0:T(4,128)S(1)}, f32[6,4,1,128]{3,1,2,0:T(4,128)S(1)}, u32[]{:S(2)}, u32[]{:S(2)}) collective-permute-start(f32[6,4,1,128]{3,1,2,0:T(4,128)S(1)} %bitcast.577), channel_id=1, source_target_pairs={{16,0},{32,16},{48,32},{64,48},{80,64},{96,80},{112,96},{128,112},... | collective-permute-start | bytes 36872 | tf_op jit(solution)/shard_map/ppermute | solution.py:22
  292.3 1.5 copy.389
  294.7 2.7 collective-permute-start.2
  297.3 5.9 %collective-permute-start.3 = (f32[6,4,66,1]{2,1,3,0:T(4,128)S(1)}, f32[6,4,66,1]{2,1,3,0:T(4,128)S(1)}, u32[]{:S(2)}, u32[]{:S(2)}) collective-permute-start(f32[6,4,66,1]{2,1,3,0:T(4,128)S(1)} %get-tuple-element.22), channel_id=1, source_target_pairs={{1,0},{2,1},{3,2},{4,3},{5,4},{6,5},{7,6},{8,7},{9,8},{10,9},{11,1... | collective-permute-start | bytes 19016 | tf_op jit(solution)/shard_map/ppermute | solution.py:22
  304.5 2.1 copy.430
  306.6 2.5 maximum_bitcast_fusion.2
  309.1 1.8 maximum_bitcast_fusion.3
  310.9 68.3 %all-gather.5.cloned.1.call-done = f32[3,2048,128]{1,0,2:T(4,128)} async-done(((f32[3,2048,4]{1,0,2:T(4,128)}), f32[3,2048,128]{1,0,2:T(4,128)}) %all-gather.5.cloned.1.call-update) | async-done | bytes 3145744 | tf_op jit(solution)/shard_map/all_gather | solution.py:213
  380.5 1.9 fusion.27
  383.9 1.3 fusion.441
  385.3 1.4 copy.431
  386.7 1.9 collective-permute-start.4
  389.5 2.4 collective-permute-start.5
  394.0 6.7 %collective-permute-done.5 = f32[3,4,1,128]{3,1,2,0:T(4,128)} collective-permute-done((f32[3,4,1,128]{3,1,2,0:T(4,128)}, f32[3,4,1,128]{3,1,2,0:T(4,128)}, u32[]{:S(2)}, u32[]{:S(2)}) %collective-permute-start.5) | collective-permute-done | bytes 6176 | tf_op jit(solution)/shard_map/ppermute | solution.py:19
  400.7 1.9 copy.434
  402.6 1.4 pad_maximum_fusion.22
  404.0 5.9 %collective-permute-start.6 = (f32[3,4,66,1]{2,1,3,0:T(4,128)}, f32[3,4,66,1]{2,1,3,0:T(4,128)S(1)}, u32[]{:S(2)}, u32[]{:S(2)}) collective-permute-start(f32[3,4,66,1]{2,1,3,0:T(4,128)} %get-tuple-element.25), channel_id=1, source_target_pairs={{1,0},{2,1},{3,2},{4,3},{5,4},{6,5},{7,6},{8,7},{9,8},{10,9},{11,1... | collective-permute-start | bytes 9512 | tf_op jit(solution)/shard_map/ppermute | solution.py:22
  409.9 2.1 collective-permute-start.7
  414.2 4.1 collective-permute-done.7
  418.4 4.8 %fusion.11 = (f32[3,4,64,128]{2,1,3,0:T(4,128)S(1)}, f32[3,4,64,128]{2,1,3,0:T(4,128)S(1)}) fusion(f32[3,4,66,1]{2,1,3,0:T(4,128)S(1)} %collective-permute-done.7, f32[3,4,1,128]{2,1,3,0:T(4,128)S(1)} %copy.432, f32[3,4,64,128]{2,1,3,0:T(4,128)S(1)} %fusion.14, f32[3,4,1,128]{2,1,3,0:T(4,128)} %copy.434, f32[3,4,66,1]{2,1,3,0:T(4,128)S(1)} %collective-permute-done.6), kind=kLoop, calls=%fused_computation.155 | loop fusion | flops 1179648 | bytes 1198272 | tf_op jit(solution)/shard_map/mul | solution.py:75
  427.6 1.4 copy.443
  (210 shorter events, 73.3 us)
Async XLA Ops:
  7.2 109.5 %all-gather.3.cloned.1.call-start = ((), (), s32[]{:S(2)}) async-start(), calls=%async_computation.4 | async-start | bytes 3244032 | tf_op jit(solution)/shard_map/all_gather | solution.py:154
  123.1 7.7 %copy-start.20 = (f32[7,4,1,16,128]{4,3,2,1,0:T(8,128)S(1)}, f32[7,4,1,16,128]{4,3,2,1,0:T(8,128)}, u32[]{:S(2)}) copy-start(f32[7,4,1,16,128]{4,3,2,1,0:T(8,128)} %param.8) | copy-start | bytes 688132
  124.5 13.0 %all-to-all-start = ((f32[2,3,64,128]{3,0,1,2:T(2,128)}), f32[2,3,64,128]{3,0,1,2:T(2,128)S(1)}, u32[]{:S(2)}, u32[]{:S(2)}) async-start(f32[2,3,64,128]{3,0,1,2:T(2,128)} %copy.394), calls=%async_computation | async-start | bytes 393216 | tf_op jit(solution)/shard_map/all_to_all | solution.py:57
  156.8 7.9 %copy-start.16 = (f32[4,16,128,6]{2,1,0,3:T(8,128)S(1)}, f32[4,16,128,6]{2,1,0,3:T(8,128)}, u32[]{:S(2)}) copy-start(f32[4,16,128,6]{2,1,0,3:T(8,128)} %slice_bitcast_fusion.16) | copy-start | bytes 589828
  156.8 7.9 %copy-start.5 = (f32[6,2,3,4,1,16,128]{6,5,4,3,2,1,0:T(8,128)S(1)}, f32[6,2,3,4,1,16,128]{6,5,4,3,2,1,0:T(8,128)}, u32[]{:S(2)}) copy-start(f32[6,2,3,4,1,16,128]{6,5,4,3,2,1,0:T(8,128)} %param.7) | copy-start | bytes 3538948
  158.7 21.7 %all-to-all-start.1 = ((f32[32,1,1536]{2,1,0:T(1,128)}), f32[32,1,1536]{2,1,0:T(1,128)S(1)}, u32[]{:S(2)}, u32[]{:S(2)}) async-start(f32[32,1,1536]{2,1,0:T(1,128)} %reshape.268), calls=%async_computation.1 | async-start | bytes 393216 | tf_op jit(solution)/shard_map/all_to_all | solution.py:62
  246.2 0.7 copy-start.22
  246.2 0.7 copy-start.23
  259.3 2.6 copy-start.17
  262.8 12.4 %all-to-all-start.3 = ((f32[2,3,64,128]{3,0,1,2:T(2,128)}), f32[2,3,64,128]{3,0,1,2:T(2,128)S(1)}, u32[]{:S(2)}, u32[]{:S(2)}) async-start(f32[2,3,64,128]{3,0,1,2:T(2,128)} %copy.417), calls=%async_computation.3 | async-start | bytes 393216 | tf_op jit(solution)/shard_map/all_to_all | solution.py:57
  268.5 110.7 %all-gather.5.cloned.1.call-start = ((), (), s32[]{:S(2)}) async-start(), calls=%async_computation.5 | async-start | bytes 4325376 | tf_op jit(solution)/shard_map/all_gather | solution.py:213
  276.6 2.6 copy-start.15
  279.2 12.3 %collective-permute-start = (f32[6,4,1,128]{3,1,2,0:T(4,128)S(1)}, f32[6,4,1,128]{3,1,2,0:T(4,128)S(1)}, u32[]{:S(2)}, u32[]{:S(2)}) collective-permute-start(f32[6,4,1,128]{3,1,2,0:T(4,128)S(1)} %bitcast.578), channel_id=1, source_target_pairs={{0,16},{16,32},{32,48},{48,64},{64,80},{80,96},{96,112},{112,128},... | collective-permute-start | bytes 36872 | tf_op jit(solution)/shard_map/ppermute | solution.py:19
  281.1 11.2 %collective-permute-start.1 = (f32[6,4,1,128]{3,1,2,0:T(4,128)S(1)}, f32[6,4,1,128]{3,1,2,0:T(4,128)S(1)}, u32[]{:S(2)}, u32[]{:S(2)}) collective-permute-start(f32[6,4,1,128]{3,1,2,0:T(4,128)S(1)} %bitcast.577), channel_id=1, source_target_pairs={{16,0},{32,16},{48,32},{64,48},{80,64},{96,80},{112,96},{128,112},... | collective-permute-start | bytes 36872 | tf_op jit(solution)/shard_map/ppermute | solution.py:22
  294.7 12.0 %collective-permute-start.2 = (f32[6,4,66,1]{2,1,3,0:T(4,128)S(1)}, f32[6,4,66,1]{2,1,3,0:T(4,128)S(1)}, u32[]{:S(2)}, u32[]{:S(2)}) collective-permute-start(f32[6,4,66,1]{2,1,3,0:T(4,128)S(1)} %get-tuple-element.21), channel_id=1, source_target_pairs={{0,1},{1,2},{2,3},{3,4},{4,5},{5,6},{6,7},{7,8},{8,9},{9,10},{10,1... | collective-permute-start | bytes 19016 | tf_op jit(solution)/shard_map/ppermute | solution.py:19
  297.3 9.3 %collective-permute-start.3 = (f32[6,4,66,1]{2,1,3,0:T(4,128)S(1)}, f32[6,4,66,1]{2,1,3,0:T(4,128)S(1)}, u32[]{:S(2)}, u32[]{:S(2)}) collective-permute-start(f32[6,4,66,1]{2,1,3,0:T(4,128)S(1)} %get-tuple-element.22), channel_id=1, source_target_pairs={{1,0},{2,1},{3,2},{4,3},{5,4},{6,5},{7,6},{8,7},{9,8},{10,9},{11,1... | collective-permute-start | bytes 19016 | tf_op jit(solution)/shard_map/ppermute | solution.py:22
  306.6 2.5 copy-start
  310.9 71.5 %copy-start.3 = (f32[4,66,130]{1,0,2:T(4,128)S(1)}, f32[4,66,130]{1,0,2:T(4,128)}, u32[]{:S(2)}) copy-start(f32[4,66,130]{1,0,2:T(4,128)} %get-tuple-element.16) | copy-start | bytes 411844
  310.9 71.5 %copy-start.4 = (f32[4,66,130]{1,0,2:T(4,128)S(1)}, f32[4,66,130]{1,0,2:T(4,128)}, u32[]{:S(2)}) copy-start(f32[4,66,130]{1,0,2:T(4,128)} %get-tuple-element.18) | copy-start | bytes 411844
  310.9 71.5 %copy-start.11 = (f32[3,64,128]{1,0,2:T(4,128)S(1)}, f32[3,64,128]{1,0,2:T(4,128)}, u32[]{:S(2)}) copy-start(f32[3,64,128]{1,0,2:T(4,128)} %get-tuple-element.31) | copy-start | bytes 294916
  310.9 71.5 %copy-start.12 = (f32[3,64,128]{1,0,2:T(4,128)S(1)}, f32[3,64,128]{1,0,2:T(4,128)}, u32[]{:S(2)}) copy-start(f32[3,64,128]{1,0,2:T(4,128)} %get-tuple-element.34) | copy-start | bytes 294916
  310.9 71.5 %copy-start.13 = (f32[3,64,128]{1,0,2:T(4,128)S(1)}, f32[3,64,128]{1,0,2:T(4,128)}, u32[]{:S(2)}) copy-start(f32[3,64,128]{1,0,2:T(4,128)} %get-tuple-element.35) | copy-start | bytes 294916
  310.9 71.5 %copy-start.14 = (f32[3,64,128]{1,0,2:T(4,128)S(1)}, f32[3,64,128]{1,0,2:T(4,128)}, u32[]{:S(2)}) copy-start(f32[3,64,128]{1,0,2:T(4,128)} %get-tuple-element.36) | copy-start | bytes 294916
  382.4 1.1 copy-start.1
  385.3 6.6 %copy-start.18 = (f32[3,64,128]{2,1,0:T(8,128)S(1)}, f32[3,64,128]{2,1,0:T(8,128)}, u32[]{:S(2)}) copy-start(f32[3,64,128]{2,1,0:T(8,128)} %param.6) | copy-start | bytes 294916
  385.3 7.6 %copy-start.21 = (f32[4,64,128]{2,1,0:T(8,128)S(1)}, f32[4,64,128]{2,1,0:T(8,128)}, u32[]{:S(2)}) copy-start(f32[4,64,128]{2,1,0:T(8,128)} %param.11) | copy-start | bytes 393220
  386.7 7.0 %collective-permute-start.4 = (f32[3,4,1,128]{3,1,2,0:T(4,128)S(1)}, f32[3,4,1,128]{3,1,2,0:T(4,128)S(1)}, u32[]{:S(2)}, u32[]{:S(2)}) collective-permute-start(f32[3,4,1,128]{3,1,2,0:T(4,128)S(1)} %copy.431), channel_id=1, source_target_pairs={{16,0},{32,16},{48,32},{64,48},{80,64},{96,80},{112,96},{128,112},... | collective-permute-start | bytes 18440 | tf_op jit(solution)/shard_map/ppermute | solution.py:22
  389.5 11.3 %collective-permute-start.5 = (f32[3,4,1,128]{3,1,2,0:T(4,128)}, f32[3,4,1,128]{3,1,2,0:T(4,128)}, u32[]{:S(2)}, u32[]{:S(2)}) collective-permute-start(f32[3,4,1,128]{3,1,2,0:T(4,128)} %copy.433), channel_id=1, source_target_pairs={{0,16},{16,32},{32,48},{48,64},{64,80},{80,96},{96,112},{112,128},... | collective-permute-start | bytes 18440 | tf_op jit(solution)/shard_map/ppermute | solution.py:19
  404.0 10.2 %collective-permute-start.6 = (f32[3,4,66,1]{2,1,3,0:T(4,128)}, f32[3,4,66,1]{2,1,3,0:T(4,128)S(1)}, u32[]{:S(2)}, u32[]{:S(2)}) collective-permute-start(f32[3,4,66,1]{2,1,3,0:T(4,128)} %get-tuple-element.25), channel_id=1, source_target_pairs={{1,0},{2,1},{3,2},{4,3},{5,4},{6,5},{7,6},{8,7},{9,8},{10,9},{11,1... | collective-permute-start | bytes 9512 | tf_op jit(solution)/shard_map/ppermute | solution.py:22
  409.9 8.4 %collective-permute-start.7 = (f32[3,4,66,1]{2,1,3,0:T(4,128)}, f32[3,4,66,1]{2,1,3,0:T(4,128)S(1)}, u32[]{:S(2)}, u32[]{:S(2)}) collective-permute-start(f32[3,4,66,1]{2,1,3,0:T(4,128)} %get-tuple-element.26), channel_id=1, source_target_pairs={{0,1},{1,2},{2,3},{3,4},{4,5},{5,6},{6,7},{7,8},{8,9},{9,10},{10,1... | collective-permute-start | bytes 9512 | tf_op jit(solution)/shard_map/ppermute | solution.py:19
  414.2 8.9 %copy-start.2 = (f32[3,64,128]{1,0,2:T(4,128)S(1)}, f32[3,64,128]{1,0,2:T(4,128)}, u32[]{:S(2)}) copy-start(f32[3,64,128]{1,0,2:T(4,128)} %get-tuple-element.46) | copy-start | bytes 294916
  423.4 1.0 copy-start.8
  423.4 1.0 copy-start.9
  423.4 1.0 copy-start.19
  423.6 1.1 copy-start.6
  423.6 1.1 copy-start.7
  425.5 1.0 copy-start.10
Sparse Core Ops, SparseCore 0:
  11.4 105.2 all-gather.2
  279.3 99.8 all-gather.4
